TPU v7x, 32 devices: a whole 2x2x4 slice. The times are simulated.
32 devices in a mesh: groups: 2 (over y), pair: 4 (over x, core), feat: 4 (over z).
Axes of the slice: x: 2, y: 2, z: 4, core: 2. Of those that a mesh axis runs over, the one named last changes fastest.
Arguments:
- queries: bfloat16 [512, 458752], P(('groups', 'pair'), 'feat'), parts along dimension 0, may hold values from -6 to 6
- store: bfloat16 [1536, 458752], P(('groups', 'pair'), 'feat'), parts along dimension 0, may hold values from -6 to 6
- stored_norms: float32 [1536], P('groups'), parts along dimension 0, may hold values from 0.5 to 5
- norm_index: int32 [1536], P(('groups', 'pair')), parts along dimension 0, may hold values from 0 to 767
- visit_order: int32 [512], P('groups'), parts along dimension 0, may hold values from 0 to 255, each once
Outputs:
- influence: float32 [512, 768], P(('groups', 'feat'), 'pair'), parts along dimension 0
There are 2 independent parts, one for each index of `groups`. A program takes and returns all parts, laid end to end along the dimension named above; each array names one. Nothing has to cross between parts.
Inputs may be any that keep to these rules, and one draw needn't show every extreme that they name: visit_order is a permutation of the query indices.
All inputs are finite; a program needn't handle non-finite values.
Results may differ from a plain program's by a relative error of at most 0.0003.
Values may be sent and summed in bfloat16 or wider, within the bound.
A program may use at most 192 MiB of HBM per device.

v0:
```python
import jax
import jax.numpy as jnp
from jax import lax
from jax.sharding import PartitionSpec as P


def block_terms(store, piece):
    block_scores = lax.dot_general(
        piece, store, (((1,), (1,)), ((), ())), preferred_element_type=jnp.float32
    )
    block_squares = jnp.einsum("qf,qf->q", piece, piece, preferred_element_type=jnp.float32)
    return (block_scores, block_squares)


def shards(queries, store, stored_norms, norm_index, visit_order):
    gathered = lax.all_gather(queries, "pair", axis=0, tiled=True)
    partial_value, squares = block_terms(store, gathered)
    ordered = jnp.take(partial_value, visit_order, axis=0)
    ordered_squares = jnp.take(squares, visit_order)
    shares, mine_squares = (
        lax.psum_scatter(ordered, "feat", scatter_dimension=0, tiled=True),
        lax.psum_scatter(ordered_squares, "feat", scatter_dimension=0, tiled=True),
    )
    query_norms = jnp.sqrt(mine_squares + 1e-06)
    pair_norms = jnp.take(stored_norms, norm_index)
    return shares / (query_norms[:, None] * pair_norms[None, :])


def solution(mesh):
    return jax.shard_map(
        shards,
        mesh=mesh,
        in_specs=(
            P(("groups", "pair"), "feat"),
            P(("groups", "pair"), "feat"),
            P("groups"),
            P(("groups", "pair")),
            P("groups"),
        ),
        out_specs=P(("groups", "feat"), "pair"),
        check_vma=False,
    )
```

profile of v0, /device:TPU:0, one launch (start us, length us, event | category | flops | bytes accessed | tf_op | source)
XLA Modules:
  0.0 441.9 jit_solution(5116390400080667700)
XLA Ops:
  6.5 0.0 copy-start
  6.5 0.0 all-gather.2.cloned.1.call-start
  6.5 0.7 all-gather.2.cloned.1.call-update
  7.3 0.0 reduce-scatter.2.cloned.1.call-start
  7.3 0.7 compare_select_fusion.1
  8.0 0.7 compare_select_fusion
  8.7 349.0 %all-gather.2.cloned.1.call-done = bf16[256,114688]{1,0:T(8,128)(2,1)} async-done(((bf16[64,114688]{1,0:T(8,128)(2,1)}), bf16[256,114688]{1,0:T(8,128)(2,1)}) %all-gather.2.cloned.1.call-update) | async-done | bytes 58720272 | tf_op jit(solution)/shard_map/all_gather | solution.py:16
  357.7 18.5 %fusion = f32[256]{0:T(256)S(1)} fusion(bf16[256,114688]{1,0:T(8,128)(2,1)} %all-gather.2.cloned.1.call-done), kind=kLoop, calls=%fused_computation.4 | loop fusion | flops 88080128 | bytes 58721280 | tf_op jit(solution)/shard_map/qf,qf->q/dot_general | solution.py:11
  376.2 2.0 gather_fusion.1
  378.1 0.0 copy-start.1
  378.2 0.0 copy-start.3
  378.2 0.0 copy-start.2
  378.2 33.7 %fusion.2 = f32[256,192]{1,0:T(8,128)S(1)} fusion(bf16[256,114688]{1,0:T(8,128)(2,1)} %all-gather.2.cloned.1.call-done, bf16[192,114688]{1,0:T(8,128)(2,1)} %param.6), kind=kOutput, calls=%fused_computation.16 | convolution fusion | flops 11274289152 | bytes 102957056 | tf_op jit(solution)/shard_map/dot_general | solution.py:8
  411.9 1.0 gather_fusion
  412.9 0.0 copy-done.1
  412.9 0.8 broadcast_select_fusion
  413.7 0.0 reduce-scatter.2.cloned.1.call-update
  413.7 0.0 copy-done.3
  413.7 0.6 dynamic-slice
  415.0 0.0 copy-done
  415.0 1.2 gather_fusion.2
  416.2 0.0 copy-done.2
  416.2 11.7 %all-reduce = f32[256]{0:T(256)S(1)} all-reduce(f32[256]{0:T(256)S(1)} %get-tuple-element.5), channel_id=3, replica_groups=mesh['groups'=2,'pair'=4,'feat'=4] {'feat'}, use_global_device_ids=true, to_apply=%region_1.2.clone | all-reduce | flops 256 | bytes 2048
  427.9 0.1 fusion.1
  428.0 5.5 %reduce-scatter.2.cloned.1.call-done = f32[64,192]{1,0:T(8,128)} async-done(((f32[256,192]{1,0:T(8,128)}), f32[64,192]{1,0:T(8,128)}) %reduce-scatter.2.cloned.1.call-update) | async-done | bytes 49168 | tf_op jit(solution)/shard_map/reduce_scatter | solution.py:21
  433.5 1.6 multiply_divide_fusion
  (4 shorter events, 0.0 us)
Async XLA Ops:
  6.5 408.4 %copy-start = (f32[768]{0:T(1024)S(1)}, f32[768]{0:T(1024)}, u32[]{:S(2)}) copy-start(f32[768]{0:T(1024)} %param.7) | copy-start | bytes 9220
  6.5 351.1 %all-gather.2.cloned.1.call-start = ((), (), s32[]{:S(2)}) async-start(), calls=%async_computation.1 | async-start | bytes 73400320 | tf_op jit(solution)/shard_map/all_gather | solution.py:16
  7.3 426.2 %reduce-scatter.2.cloned.1.call-start = ((), (), s32[]{:S(2)}) async-start(), calls=%async_computation.2 | async-start | bytes 327680 | tf_op jit(solution)/shard_map/reduce_scatter | solution.py:21
  378.1 34.7 %copy-start.1 = (s32[256]{0:T(256)S(1)}, s32[256]{0:T(256)}, u32[]{:S(2)}) copy-start(s32[256]{0:T(256)} %param.9) | copy-start | bytes 3076
  378.2 35.6 %copy-start.3 = (u32[32]{0:T(128)S(1)}, u32[32]{0:T(128)}, u32[]{:S(2)}) copy-start(u32[32]{0:T(128)} %constant.47) | copy-start | bytes 388
  378.2 38.0 %copy-start.2 = (s32[192]{0:T(256)S(1)}, s32[192]{0:T(256)}, u32[]{:S(2)}) copy-start(s32[192]{0:T(256)} %param.8) | copy-start | bytes 2308
Sparse Core Ops, SparseCore 0:
  8.9 348.6 all-gather.1
  413.8 19.6 reduce-scatter.1
where the time goes:
time: 442 us
  waiting for transfers between devices  355 us (80%)
  matrix products  33.7 us (8%)
  other arithmetic  22.3 us (5%)
  between operations  14.2 us (3%)
  blocking collectives  11.7 us (3%)
  local copies, waits for them, and re-layouts  4.7 us (1%)
    all_gather x1, waiting for transfers between devices, shards(): gathered = lax.all_gather(queries, 'pair', axis=0, tiled=True)  349 us
    dot_general x1, matrix products, block_terms(): lax.dot_general(piece, store, (((1,), (1,)), ((), ())), preferred_element...  33.7 us
    dot_general x1, other arithmetic, block_terms(): jnp.einsum('qf,qf->q', piece, piece, preferred_element_type=jnp.float32)  18.5 us
    unnamed x1, blocking collectives  11.7 us
  transfers between devices with their start and end apart: 2, of which 2 were waited for; matrix products, arithmetic and copies ran while one was open for 1% of the time, Pallas kernels for 0%

commit v1 on v0

v1 whole, which is shorter than its diff:
```python
import functools

import jax
import jax.numpy as jnp
from jax import lax
from jax.experimental import pallas as pl
from jax.experimental.pallas import tpu as pltpu
from jax.sharding import PartitionSpec as P

MESH = pl.DeviceIdType.MESH
LANES = 128
TAIL_ROWS = 16
BUFFERS = 4
AHEAD = 12
EXACT = lax.Precision.HIGHEST


def chunk_width(features):
    tiles = features // LANES
    best = max(t for t in range(1, 17) if tiles % t == 0)
    return best * LANES


def kernel(
    chips, feats, width, segments,
    queries, store, table, index, visit, out,
    sib_land, x_land, xs_land, store_buf, own_buf,
    acc_first, acc_last, sq_first, sq_last, full, order, ordered, red_first, red_last, norm,
    store_sem, own_sem, sib_send, sib_recv, x_send, x_recv, xs_send, xs_recv, z_send, z_recv,
):
    rows, features = queries.shape
    pairs = store.shape[0]
    padded = store_buf.shape[1]
    steps = features // width
    nq = full.shape[0]
    owned = nq // feats
    me = lax.axis_index("pair")
    core = lax.rem(me, 2)
    chip = lax.div(me, 2)
    z = lax.axis_index("feat")
    sibling = me + 1 - 2 * core

    def at(i):
        return pl.ds(pl.multiple_of(i * width, width), width)

    def chip_by(j):
        return lax.rem(chip + j + chips, chips)

    barrier = pltpu.get_barrier_semaphore()
    pl.semaphore_signal(barrier, inc=1, device_id={"pair": sibling}, device_id_type=MESH)
    for j in range(1, chips):
        pl.semaphore_signal(
            barrier, inc=1, device_id={"pair": chip_by(j) * 2 + core}, device_id_type=MESH
        )
    for k in range(1, feats):
        pl.semaphore_signal(
            barrier, inc=1, device_id={"feat": lax.rem(z + k, feats)}, device_id_type=MESH
        )
    pl.semaphore_wait(barrier, chips + feats - 1)

    def sib_copy(i):
        return pltpu.make_async_remote_copy(
            queries.at[:, at(i)], sib_land.at[:, at(i)], sib_send.at[i], sib_recv.at[i],
            device_id={"pair": sibling}, device_id_type=MESH,
        )

    def x_copy(s, j, i):
        part = pl.ds(*segments[s])
        return pltpu.make_async_remote_copy(
            queries.at[part, at(i)], x_land.at[j - 1, part, at(i)],
            x_send.at[s, j - 1, i], x_recv.at[s, j - 1, i],
            device_id={"pair": chip_by(j) * 2 + core}, device_id_type=MESH,
        )

    def xs_copy(s, j, i):
        part = pl.ds(*segments[s])
        return pltpu.make_async_remote_copy(
            x_land.at[j - 1, part, at(i)], xs_land.at[j - 1, part, at(i)],
            xs_send.at[s, j - 1, i], xs_recv.at[s, j - 1, i],
            device_id={"pair": sibling}, device_id_type=MESH,
        )

    def store_load(i):
        slot = lax.rem(i, BUFFERS)
        return pltpu.make_async_copy(
            store.at[:, at(i)], store_buf.at[slot, pl.ds(0, pairs)], store_sem.at[slot]
        )

    def own_load(i):
        slot = lax.rem(i, BUFFERS)
        return pltpu.make_async_copy(queries.at[:, at(i)], own_buf.at[slot], own_sem.at[slot])

    def send(s, i):
        for j in range(1, chips):
            x_copy(s, j, i).start()
        if s == 0:
            sib_copy(i).start()

    @pl.loop(0, min(AHEAD, steps))
    def _(i):
        send(0, i)

    for i in range(min(BUFFERS - 1, steps)):
        own_load(i).start()
        store_load(i).start()

    store_buf[:, pairs:, :] = jnp.zeros((BUFFERS, padded - pairs, width), store_buf.dtype)
    entries = table.shape[1]
    chosen = (
        lax.broadcasted_iota(jnp.int32, (entries, pairs), 0) == index[...]
    ).astype(jnp.float32)
    norm[...] = jnp.dot(
        jnp.broadcast_to(table[...], (8, entries)), chosen,
        precision=EXACT, preferred_element_type=jnp.float32,
    )
    order[...] = (
        lax.broadcasted_iota(jnp.int32, (nq, nq), 0) == visit[...]
    ).astype(jnp.float32).T
    for ref in (acc_first, acc_last, sq_first, sq_last, full):
        ref[...] = jnp.zeros_like(ref)

    def run(s, acc, sq):
        part = pl.ds(*segments[s])

        @pl.loop(0, steps + 1)
        def _(i):
            @pl.when(i < steps)
            def _():
                for j in range(1, chips):
                    x_copy(s, j, i).wait_recv()
                    xs_copy(s, j, i).start()

            @pl.when(i + AHEAD < steps)
            def _():
                send(s, i + AHEAD)

            if s + 1 < len(segments):
                @pl.when((i + AHEAD >= steps) & (i < steps) & (i + AHEAD - steps < steps))
                def _():
                    send(s + 1, i + AHEAD - steps)

            @pl.when(i >= 1)
            def _():
                n = i - 1
                slot = lax.rem(n, BUFFERS)

                @pl.when(n + BUFFERS - 1 < steps)
                def _():
                    if s == 0:
                        own_load(n + BUFFERS - 1).start()
                    store_load(n + BUFFERS - 1).start()

                store_load(n).wait()
                if s == 0:
                    own_load(n).wait()
                    sib_copy(n).wait_recv()
                for j in range(1, chips):
                    xs_copy(s, j, n).wait_recv()
                pieces = []
                if s == 0:
                    pieces += [own_buf[slot], sib_land[:, at(n)]]
                for j in range(1, chips):
                    pieces += [x_land[j - 1, part, at(n)], xs_land[j - 1, part, at(n)]]
                piece = jnp.concatenate(pieces, axis=0)
                acc[...] += lax.dot_general(
                    piece, store_buf[slot], (((1,), (1,)), ((), ())),
                    preferred_element_type=jnp.float32,
                )
                total = sq[...]
                for t in range(width // LANES):
                    wide = piece[:, t * LANES : (t + 1) * LANES].astype(jnp.float32)
                    total += wide * wide
                sq[...] = total

    def joined(acc, sq):
        square = jnp.sum(sq[...], axis=1, keepdims=True)
        lane = lax.broadcasted_iota(jnp.int32, acc.shape, 1)
        return jnp.where(lane < pairs, acc[...], square)

    def blocks(s):
        start, count = segments[s]
        found = []
        if s == 0:
            found += [(me, 0, rows), (sibling, 0, rows)]
        for j in range(1, chips):
            source = chip_by(-j) * 2 + core
            found += [(source, start, count), (source + 1 - 2 * core, start, count)]
        return found

    def place(s, value):
        offset = 0
        for block, start, count in blocks(s):
            full[pl.ds(pl.multiple_of(block * rows + start, 16), count)] = value[
                offset : offset + count
            ]
            offset += count

    mine = pl.ds(pl.multiple_of(z * owned, 8), owned)

    def first_copy(k):
        target = lax.rem(z + k, feats)
        return pltpu.make_async_remote_copy(
            ordered.at[pl.ds(pl.multiple_of(target * owned, 8), owned)], red_first.at[k],
            z_send.at[0, k], z_recv.at[0, k],
            device_id={"feat": target}, device_id_type=MESH,
        )

    def last_copy(k):
        return pltpu.make_async_remote_copy(
            red_last.at[0], red_last.at[k], z_send.at[1, k], z_recv.at[1, k],
            device_id={"feat": lax.rem(z + k, feats)}, device_id_type=MESH,
        )

    run(0, acc_first, sq_first)
    for i in range(min(BUFFERS - 1, steps)):
        store_load(i).start()
    place(0, joined(acc_first, sq_first))
    ordered[...] = jnp.dot(
        order[...], full[...], precision=EXACT, preferred_element_type=jnp.float32
    )
    for k in range(1, feats):
        first_copy(k).start()

    run(1, acc_last, sq_last)
    red_last[0] = joined(acc_last, sq_last)
    for k in range(1, feats):
        last_copy(k).start()

    @pl.loop(0, steps)
    def _(i):
        sib_copy(i).wait_send()
        for s in range(len(segments)):
            for j in range(1, chips):
                x_copy(s, j, i).wait_send()
                xs_copy(s, j, i).wait_send()

    total = ordered[mine]
    for k in range(1, feats):
        first_copy(k).wait()
        total += red_first[k]
    full[...] = jnp.zeros_like(full)
    last = red_last[0]
    for k in range(1, feats):
        last_copy(k).wait()
        last += red_last[k]
    place(1, last)
    total += jnp.dot(order[mine], full[...], precision=EXACT, preferred_element_type=jnp.float32)
    query_norm = jnp.sqrt(total[:, pairs : pairs + 1] + 1e-06)
    out[...] = total[:, :pairs] / (query_norm * norm[0:1])


def shards(chips, feats, queries, store, stored_norms, norm_index, visit_order):
    rows, features = queries.shape
    pairs = store.shape[0]
    nq = visit_order.shape[0]
    padded = (pairs // LANES + 1) * LANES
    width = chunk_width(features)
    steps = features // width
    segments = ((0, rows - TAIL_ROWS), (rows - TAIL_ROWS, TAIL_ROWS))
    others = chips - 1
    first = 2 * rows + 2 * others * (rows - TAIL_ROWS)
    last = 2 * others * TAIL_ROWS
    vmem = pl.BlockSpec(memory_space=pltpu.VMEM)
    hbm = pl.BlockSpec(memory_space=pltpu.HBM)
    dma = pltpu.SemaphoreType.DMA
    f32, bf16 = jnp.float32, jnp.bfloat16
    return pl.pallas_call(
        functools.partial(kernel, chips, feats, width, segments),
        out_shape=jax.ShapeDtypeStruct((nq // feats, pairs), f32),
        in_specs=[hbm, hbm, vmem, vmem, vmem],
        out_specs=vmem,
        scratch_shapes=[
            pltpu.VMEM((rows, features), bf16),
            pltpu.VMEM((others, rows, features), bf16),
            pltpu.VMEM((others, rows, features), bf16),
            pltpu.VMEM((BUFFERS, padded, width), bf16),
            pltpu.VMEM((BUFFERS, rows, width), bf16),
            pltpu.VMEM((first, padded), f32),
            pltpu.VMEM((last, padded), f32),
            pltpu.VMEM((first, LANES), f32),
            pltpu.VMEM((last, LANES), f32),
            pltpu.VMEM((nq, padded), f32),
            pltpu.VMEM((nq, nq), f32),
            pltpu.VMEM((nq, padded), f32),
            pltpu.VMEM((feats, nq // feats, padded), f32),
            pltpu.VMEM((feats, last, padded), f32),
            pltpu.VMEM((8, pairs), f32),
            dma((BUFFERS,)),
            dma((BUFFERS,)),
            dma((steps,)),
            dma((steps,)),
            dma((2, others, steps)),
            dma((2, others, steps)),
            dma((2, others, steps)),
            dma((2, others, steps)),
            dma((2, feats)),
            dma((2, feats)),
        ],
        compiler_params=pltpu.CompilerParams(
            collective_id=0, has_side_effects=True, vmem_limit_bytes=60 * 2**20
        ),
    )(
        queries, store, stored_norms.reshape(1, -1), norm_index.reshape(1, -1),
        visit_order.reshape(1, -1),
    )


def solution(mesh):
    return jax.shard_map(
        functools.partial(shards, mesh.shape["pair"] // 2, mesh.shape["feat"]),
        mesh=mesh,
        in_specs=(
            P(("groups", "pair"), "feat"),
            P(("groups", "pair"), "feat"),
            P("groups"),
            P(("groups", "pair")),
            P("groups"),
        ),
        out_specs=P(("groups", "feat"), "pair"),
        check_vma=False,
    )
```

time: 442 us -> 337 us (0.76)
  waiting for transfers between devices: 355 us -> 0 us
  Pallas kernels: 0 us -> 334 us
  matrix products: 33.7 us -> 0 us
  other arithmetic: 22.3 us -> 0 us
  between operations: 14.2 us -> 0.01 us
  blocking collectives: 11.7 us -> 0 us
    all_gather x1 -> x0, waiting for transfers between devices: 349 us -> none  [shards(): gathered = lax.all_gather(queries, 'pair', axis=0, tiled=True)]
    pallas_call x0 -> x1, Pallas kernels: none -> 334 us  [shards(): pl.pallas_call(functools.partial(kernel, chips, feats, width, segments),...]
    dot_general x1 -> x0, matrix products: 33.7 us -> none  [block_terms(): lax.dot_general(piece, store, (((1,), (1,)), ((), ())), preferred_element...]
    dot_general x1 -> x0, other arithmetic: 18.5 us -> none  [block_terms(): jnp.einsum('qf,qf->q', piece, piece, preferred_element_type=jnp.float32)]
    unnamed x1 -> x0, blocking collectives: 11.7 us -> none
    reduce_scatter x1 -> x0, waiting for transfers between devices: 5.53 us -> none  [shards(): lax.psum_scatter(ordered, 'feat', scatter_dimension=0, tiled=True)]
  transfers between devices with their start and end apart: 2 -> 0, of which waited for: 2 -> 0; matrix products, arithmetic and copies ran while one was open for 1% -> 0% of each run, Pallas kernels for 0% -> 0%
where the time goes in v1:
time: 337 us
  Pallas kernels  334 us (99%)
    pallas_call x1, Pallas kernels, shards(): pl.pallas_call(functools.partial(kernel, chips, feats, width, segments),...  334 us

profile of v1, /device:TPU:0, one launch (start us, length us, event | category | flops | bytes accessed | tf_op | source)
XLA Modules:
  0.0 336.9 jit_solution(11368983623205651019)
XLA Ops:
  0.0 1.3 reshape.9.table
  1.3 334.1 %shard_map.55 = f32[64,192]{1,0:T(8,128)} custom-call(bf16[64,114688]{1,0:T(8,128)(2,1)} %queries.1, bf16[192,114688]{1,0:T(8,128)(2,1)} %store.1, f32[1,768]{1,0:T(1,128)} %reshape.9.table, s32[1,192]{1,0:T(1,128)} %bitcast.2, s32[1,256]{1,0:T(1,128)} %bitcast.3), custom_call_target="tpu_custom_call" | custom-call | tf_op jit(solution)/shard_map/pallas_call | solution.py:267
  335.4 1.5 copy.7

commit v2 on v1

--- a/solution.py
+++ b/solution.py
@@ -11,18 +11,19 @@
 LANES = 128
 TAIL_ROWS = 16
 BUFFERS = 4
-AHEAD = 12
+GROUP = 4
+AHEAD = (3, 12)
 EXACT = lax.Precision.HIGHEST
 
 
 def chunk_width(features):
     tiles = features // LANES
-    best = max(t for t in range(1, 17) if tiles % t == 0)
+    best = max(t for t in range(1, 33) if tiles % t == 0)
     return best * LANES
 
 
 def kernel(
-    chips, feats, width, segments,
+    chips, feats, width, segments, groups,
     queries, store, table, index, visit, out,
     sib_land, x_land, xs_land, store_buf, own_buf,
     acc_first, acc_last, sq_first, sq_last, full, order, ordered, red_first, red_last, norm,
@@ -43,6 +44,10 @@
     def at(i):
         return pl.ds(pl.multiple_of(i * width, width), width)
 
+    def span(s, i):
+        wide = width * groups[s]
+        return pl.ds(pl.multiple_of(i * wide, width), wide)
+
     def chip_by(j):
         return lax.rem(chip + j + chips, chips)
 
@@ -60,14 +65,14 @@
 
     def sib_copy(i):
         return pltpu.make_async_remote_copy(
-            queries.at[:, at(i)], sib_land.at[:, at(i)], sib_send.at[i], sib_recv.at[i],
+            queries.at[:, span(0, i)], sib_land.at[:, span(0, i)], sib_send.at[i], sib_recv.at[i],
             device_id={"pair": sibling}, device_id_type=MESH,
         )
 
     def x_copy(s, j, i):
         part = pl.ds(*segments[s])
         return pltpu.make_async_remote_copy(
-            queries.at[part, at(i)], x_land.at[j - 1, part, at(i)],
+            queries.at[part, span(s, i)], x_land.at[j - 1, part, span(s, i)],
             x_send.at[s, j - 1, i], x_recv.at[s, j - 1, i],
             device_id={"pair": chip_by(j) * 2 + core}, device_id_type=MESH,
         )
@@ -75,7 +80,7 @@
     def xs_copy(s, j, i):
         part = pl.ds(*segments[s])
         return pltpu.make_async_remote_copy(
-            x_land.at[j - 1, part, at(i)], xs_land.at[j - 1, part, at(i)],
+            x_land.at[j - 1, part, span(s, i)], xs_land.at[j - 1, part, span(s, i)],
             xs_send.at[s, j - 1, i], xs_recv.at[s, j - 1, i],
             device_id={"pair": sibling}, device_id_type=MESH,
         )
@@ -96,23 +101,30 @@
         if s == 0:
             sib_copy(i).start()
 
-    @pl.loop(0, min(AHEAD, steps))
-    def _(i):
-        send(0, i)
+    ahead = [min(AHEAD[s], steps // groups[s]) for s in range(len(segments))]
+
+    def send_first(s):
+        @pl.loop(0, ahead[s])
+        def _(i):
+            send(s, i)
+
+    send_first(0)
 
     for i in range(min(BUFFERS - 1, steps)):
         own_load(i).start()
         store_load(i).start()
 
     store_buf[:, pairs:, :] = jnp.zeros((BUFFERS, padded - pairs, width), store_buf.dtype)
-    entries = table.shape[1]
-    chosen = (
-        lax.broadcasted_iota(jnp.int32, (entries, pairs), 0) == index[...]
-    ).astype(jnp.float32)
-    norm[...] = jnp.dot(
-        jnp.broadcast_to(table[...], (8, entries)), chosen,
-        precision=EXACT, preferred_element_type=jnp.float32,
-    )
+    lines, entries = table.shape
+    position = lax.broadcasted_iota(jnp.int32, (entries, pairs), 0)
+    norms = jnp.zeros((8, pairs), jnp.float32)
+    for line in range(lines):
+        norms += jnp.dot(
+            jnp.broadcast_to(table[line : line + 1], (8, entries)),
+            (position + line * entries == index[...]).astype(jnp.float32),
+            precision=EXACT, preferred_element_type=jnp.float32,
+        )
+    norm[...] = norms
     order[...] = (
         lax.broadcasted_iota(jnp.int32, (nq, nq), 0) == visit[...]
     ).astype(jnp.float32).T
@@ -121,23 +133,26 @@
 
     def run(s, acc, sq):
         part = pl.ds(*segments[s])
+        group = groups[s]
+        copies = steps // group
 
         @pl.loop(0, steps + 1)
         def _(i):
-            @pl.when(i < steps)
+            @pl.when((i < steps) & (lax.rem(i, group) == 0))
             def _():
+                c = lax.div(i, group)
                 for j in range(1, chips):
-                    x_copy(s, j, i).wait_recv()
-                    xs_copy(s, j, i).start()
-
-            @pl.when(i + AHEAD < steps)
-            def _():
-                send(s, i + AHEAD)
-
-            if s + 1 < len(segments):
-                @pl.when((i + AHEAD >= steps) & (i < steps) & (i + AHEAD - steps < steps))
+                    x_copy(s, j, c).wait_recv()
+                    xs_copy(s, j, c).start()
+
+                @pl.when(c + ahead[s] < copies)
                 def _():
-                    send(s + 1, i + AHEAD - steps)
+                    send(s, c + ahead[s])
+
+                if s + 1 < len(segments):
+                    @pl.when(c == copies - ahead[s])
+                    def _():
+                        send_first(s + 1)
 
             @pl.when(i >= 1)
             def _():
@@ -153,9 +168,14 @@
                 store_load(n).wait()
                 if s == 0:
                     own_load(n).wait()
-                    sib_copy(n).wait_recv()
-                for j in range(1, chips):
-                    xs_copy(s, j, n).wait_recv()
+
+                @pl.when(lax.rem(n, group) == 0)
+                def _():
+                    if s == 0:
+                        sib_copy(lax.div(n, group)).wait_recv()
+                    for j in range(1, chips):
+                        xs_copy(s, j, lax.div(n, group)).wait_recv()
+
                 pieces = []
                 if s == 0:
                     pieces += [own_buf[slot], sib_land[:, at(n)]]
@@ -211,6 +231,15 @@
             device_id={"feat": lax.rem(z + k, feats)}, device_id_type=MESH,
         )
 
+    def sent(s):
+        @pl.loop(0, steps // groups[s])
+        def _(i):
+            if s == 0:
+                sib_copy(i).wait_send()
+            for j in range(1, chips):
+                x_copy(s, j, i).wait_send()
+                xs_copy(s, j, i).wait_send()
+
     run(0, acc_first, sq_first)
     for i in range(min(BUFFERS - 1, steps)):
         store_load(i).start()
@@ -221,19 +250,13 @@
     for k in range(1, feats):
         first_copy(k).start()
 
+    sent(0)
     run(1, acc_last, sq_last)
     red_last[0] = joined(acc_last, sq_last)
     for k in range(1, feats):
         last_copy(k).start()
 
-    @pl.loop(0, steps)
-    def _(i):
-        sib_copy(i).wait_send()
-        for s in range(len(segments)):
-            for j in range(1, chips):
-                x_copy(s, j, i).wait_send()
-                xs_copy(s, j, i).wait_send()
-
+    sent(1)
     total = ordered[mine]
     for k in range(1, feats):
         first_copy(k).wait()
@@ -257,15 +280,18 @@
     width = chunk_width(features)
     steps = features // width
     segments = ((0, rows - TAIL_ROWS), (rows - TAIL_ROWS, TAIL_ROWS))
+    groups = (max(g for g in range(1, GROUP + 1) if steps % g == 0), 1)
     others = chips - 1
     first = 2 * rows + 2 * others * (rows - TAIL_ROWS)
     last = 2 * others * TAIL_ROWS
+    entries = stored_norms.shape[0]
+    line = LANES if entries % LANES == 0 else entries
     vmem = pl.BlockSpec(memory_space=pltpu.VMEM)
     hbm = pl.BlockSpec(memory_space=pltpu.HBM)
     dma = pltpu.SemaphoreType.DMA
     f32, bf16 = jnp.float32, jnp.bfloat16
     return pl.pallas_call(
-        functools.partial(kernel, chips, feats, width, segments),
+        functools.partial(kernel, chips, feats, width, segments, groups),
         out_shape=jax.ShapeDtypeStruct((nq // feats, pairs), f32),
         in_specs=[hbm, hbm, vmem, vmem, vmem],
         out_specs=vmem,
@@ -300,7 +326,7 @@
             collective_id=0, has_side_effects=True, vmem_limit_bytes=60 * 2**20
         ),
     )(
-        queries, store, stored_norms.reshape(1, -1), norm_index.reshape(1, -1),
+        queries, store, stored_norms.reshape(-1, line), norm_index.reshape(1, -1),
         visit_order.reshape(1, -1),
     )
 

time: 337 us -> 334 us (level)
  no operation moved by 1% of the time
where the time goes in v2:
time: 334 us; the launch traced here: 333 us
  Pallas kernels  332 us (99%)
    pallas_call x1, Pallas kernels, shards(): pl.pallas_call(functools.partial(kernel, chips, feats, width, segments, g...  332 us

profile of v2, /device:TPU:0, one launch (start us, length us, event | category | flops | bytes accessed | tf_op | source)
XLA Modules:
  0.0 333.4 jit_solution(3770238601414741421)
XLA Ops:
  0.0 331.9 %shard_map.55 = f32[64,192]{1,0:T(8,128)} custom-call(bf16[64,114688]{1,0:T(8,128)(2,1)} %queries.1, bf16[192,114688]{1,0:T(8,128)(2,1)} %store.1, f32[6,128]{1,0:T(8,128)} %bitcast.3, s32[1,192]{1,0:T(1,128)} %bitcast.4, s32[1,256]{1,0:T(1,128)} %bitcast.5), custom_call_target="tpu_custom_call" | custom-call | tf_op jit(solution)/shard_map/pallas_call | solution.py:293
  331.9 1.5 copy.7
